TPU v7x, 512 devices: a whole 4x4x16 slice. The times are simulated.
512 devices in a mesh: group: 16 (over y, z_lo), rows: 4 (over z_hi), tensor: 8 (over x, core).
Axes of the slice: x: 4, y: 4, z: 16 (z_hi: 4, z_lo: 4; z = z_hi * 4 + z_lo), core: 2. Of those that a mesh axis runs over, the one named last changes fastest.
Arguments:
- continuation_query: bfloat16 [2048, 4, 8192], P(('group', 'rows'), None, 'tensor'), may hold values from -24 to 24
- continuation_keys: bfloat16 [2048, 4, 1024], P(('group', 'rows'), None, 'tensor'), may hold values from -4 to 4
- continuation_values: bfloat16 [2048, 4, 1024], P(('group', 'rows'), None, 'tensor'), may hold values from -4 to 4
- prefix_cache_keys: bfloat16 [16, 1024, 1024], P('group', 'rows', 'tensor'), may hold values from -9.5 to 9.5
- prefix_cache_values: bfloat16 [16, 1024, 1024], P('group', 'rows', 'tensor'), may hold values from -4 to 4
- prefix_block_index: int32 [2048, 1], P('group'), may hold values from 0 to 15; in each aligned block of 32 rows (0 to 31, 32 to 63, ...) at most 4 rows name the same one
- prefix_lens: int32 [16], replicated, may hold values from 256 to 1024, as said below
- out_weight: bfloat16 [8192, 8192], P('tensor', 'rows'), may hold values from -1.1953125 to 1.1953125
Outputs:
- projected: bfloat16 [2048, 4, 8192], P('group', None, ('rows', 'tensor'))
Inputs may be any that keep to these rules, and one draw needn't show every extreme that they name: `prefix_lens`: one prefix block in every draw has all 1024 positions valid. `prefix_block_index`: among the 32 rows of one device no prefix block is read by more than 4 rows, and some device has one read by exactly 4.
All inputs are finite; a program needn't handle non-finite values.
Results may differ from a plain program's by a relative error of at most 0.025.
Values may be sent and summed in bfloat16 or wider, within the bound.
A program may use at most 64 MiB of HBM per device.

v0:
```python
import math

import jax
import jax.numpy as jnp
from jax import lax
from jax.sharding import PartitionSpec as P

HEAD_DIMENSION = 128


floor_score = -1e30


def partial_rows(
    query_matrix, self_keys, self_values, row_numbers, key_rows, value_rows, lengths, offset
):
    row_count_total, step_count, width_q = query_matrix.shape
    kv_heads = key_rows.shape[2] // HEAD_DIMENSION
    query_groups = width_q // (kv_heads * HEAD_DIMENSION)
    span = key_rows.shape[1]
    scale_factor = 1.0 / math.sqrt(HEAD_DIMENSION)
    reshaped_query = query_matrix.reshape(
        row_count_total, step_count, kv_heads, query_groups, HEAD_DIMENSION
    )
    selected_keys = jnp.take(key_rows, row_numbers, axis=0).reshape(
        row_count_total, span, kv_heads, HEAD_DIMENSION
    )
    selected_values = jnp.take(value_rows, row_numbers, axis=0).reshape(
        row_count_total, span, kv_heads, HEAD_DIMENSION
    )
    reshaped_keys = self_keys.reshape(row_count_total, step_count, kv_heads, HEAD_DIMENSION)
    reshaped_values = self_values.reshape(row_count_total, step_count, kv_heads, HEAD_DIMENSION)
    prefix_scores = (
        jnp.einsum(
            "bshgd,bphd->bhgsp", reshaped_query, selected_keys, preferred_element_type=jnp.float32
        )
        * scale_factor
    )
    positions = offset + jnp.arange(span, dtype=jnp.int32)
    usable = positions[None, :] < jnp.take(lengths, row_numbers)[:, None]
    usable = usable[:, None, None, None, :]
    prefix_scores = jnp.where(usable, prefix_scores, floor_score)
    own_scores = (
        jnp.einsum(
            "bshgd,bthd->bhgst", reshaped_query, reshaped_keys, preferred_element_type=jnp.float32
        )
        * scale_factor
    )
    causal = (jnp.arange(step_count)[None, :] <= jnp.arange(step_count)[:, None]) & True
    own_scores = jnp.where(causal, own_scores, floor_score)
    peak = jnp.maximum(prefix_scores.max(-1), own_scores.max(-1))
    prefix_weights = jnp.where(usable, jnp.exp(prefix_scores - peak[..., None]), 0.0)
    own_weights = jnp.where(causal, jnp.exp(own_scores - peak[..., None]), 0.0)
    total = prefix_weights.sum(-1) + own_weights.sum(-1)
    summed = jnp.einsum(
        "bhgsp,bphd->bhgsd",
        prefix_weights.astype(jnp.bfloat16),
        selected_values,
        preferred_element_type=jnp.float32,
    )
    summed = summed + jnp.einsum(
        "bhgst,bthd->bhgsd",
        own_weights.astype(jnp.bfloat16),
        reshaped_values,
        preferred_element_type=jnp.float32,
    )
    return (peak, total, summed)


def attend_rows(
    query_matrix, self_keys, self_values, row_numbers, key_rows, value_rows, lengths, offset
):
    row_count_total = query_matrix.shape[0]
    block_of_rows = row_count_total // math.gcd(row_count_total, 4)
    count_of_blocks = row_count_total // block_of_rows

    def one_block(items):
        return partial_rows(
            items[0], items[1], items[2], items[3], key_rows, value_rows, lengths, offset
        )

    stacked_tensors = (
        query_matrix.reshape((count_of_blocks, block_of_rows) + query_matrix.shape[1:]),
        self_keys.reshape((count_of_blocks, block_of_rows) + self_keys.shape[1:]),
        self_values.reshape((count_of_blocks, block_of_rows) + self_values.shape[1:]),
        row_numbers.reshape(count_of_blocks, block_of_rows),
    )
    results = lax.map(one_block, stacked_tensors)
    return tuple((piece.reshape((row_count_total,) + piece.shape[2:]) for piece in results))


def finalize(total, summed):
    row_count_total, kv_heads, query_groups, step_count, head_size = summed.shape
    normalized = summed / total[..., None]
    normalized = normalized.transpose(0, 3, 1, 2, 4).reshape(
        row_count_total, step_count, kv_heads * query_groups * head_size
    )
    return normalized.astype(jnp.bfloat16)


def local(
    continuation_query,
    continuation_keys,
    continuation_values,
    prefix_cache_keys,
    prefix_cache_values,
    prefix_block_index,
    prefix_lens,
    out_weight,
):
    prefix_block_index = prefix_block_index.reshape(-1)
    rows_here = continuation_query.shape[0]
    row_index = lax.axis_index("rows")
    quarter = prefix_cache_keys.shape[1]
    width_kv = prefix_cache_keys.shape[2]
    flat_keys = prefix_cache_keys.reshape(quarter, width_kv)
    flat_values = prefix_cache_values.reshape(quarter, width_kv)
    keys_all, values_all = (
        lax.all_gather(flat_keys, ("group", "rows"), axis=0, tiled=True),
        lax.all_gather(flat_values, ("group", "rows"), axis=0, tiled=True),
    )
    keys_all = keys_all.reshape(-1, quarter * lax.axis_size("rows"), width_kv)
    values_all = values_all.reshape(-1, quarter * lax.axis_size("rows"), width_kv)
    own_ids = lax.dynamic_slice_in_dim(prefix_block_index, row_index * rows_here, rows_here)
    peak, total, summed = attend_rows(
        continuation_query,
        continuation_keys,
        continuation_values,
        own_ids,
        keys_all,
        values_all,
        prefix_lens,
        0,
    )
    attended_own = finalize(total, summed)
    attended = lax.all_gather(attended_own, "rows", axis=0, tiled=True)
    flattened = attended.reshape(-1, attended.shape[2])
    head_terms = jnp.dot(flattened, out_weight, preferred_element_type=jnp.float32)
    head_terms = head_terms.reshape(attended.shape[0], attended.shape[1], out_weight.shape[1])
    return lax.psum_scatter(
        head_terms.astype(jnp.bfloat16), "tensor", scatter_dimension=2, tiled=True
    )


def solution(mesh):
    return jax.shard_map(
        local,
        mesh=mesh,
        in_specs=(
            P(("group", "rows"), None, "tensor"),
            P(("group", "rows"), None, "tensor"),
            P(("group", "rows"), None, "tensor"),
            P("group", "rows", "tensor"),
            P("group", "rows", "tensor"),
            P("group", None),
            P(),
            P("tensor", "rows"),
        ),
        out_specs=P("group", None, ("rows", "tensor")),
        check_vma=False,
    )
```

profile of v0, /device:TPU:1, one launch (start us, length us, event | category | flops | bytes accessed | tf_op | source)
XLA Modules:
  0.0 1025.8 jit_solution(14347880810243237226)
XLA Ops:
  6.5 0.0 copy-start
  6.5 0.0 all-gather.8.cloned.1.call-start
  6.5 0.7 all-gather.8.cloned.1.call-update
  7.3 0.0 all-gather.10.cloned.1.call-start
  7.3 0.7 all-gather.10.cloned.1.call-update
  8.0 0.0 all-gather.6.cloned.1.call-start
  8.1 0.1 dynamic-slice_reduce_fusion
  8.2 0.1 reshape.199
  8.3 374.7 %all-gather.8.cloned.1.call-done = bf16[1,16384,128]{2,1,0:T(8,128)(2,1)} async-done(((bf16[1,256,128]{2,1,0:T(8,128)(2,1)}), bf16[1,16384,128]{2,1,0:T(8,128)(2,1)}) %all-gather.8.cloned.1.call-update) | async-done | bytes 4194320 | tf_op jit(solution)/shard_map/all_gather | solution.py:119
  383.0 422.9 %all-gather.10.cloned.1.call-done = bf16[1,16384,128]{2,1,0:T(8,128)(2,1)} async-done(((bf16[1,256,128]{2,1,0:T(8,128)(2,1)}), bf16[1,16384,128]{2,1,0:T(8,128)(2,1)}) %all-gather.10.cloned.1.call-update) | async-done | bytes 4194320 | tf_op jit(solution)/shard_map/all_gather | solution.py:120
  805.9 54.1 %while.12 = (s32[]{:T(128)}, f32[4,8,1,8,4]{3,4,2,1,0:T(4,128)S(1)}, f32[4,8,1,8,4,128]{5,3,4,1,2,0:T(8,128)}, s32[4,8]{1,0:T(4,128)S(1)}, s32[16]{0:T(128)}, /*...) while((s32[]{:T(128)}, ...), condition=%wide.region_5.7_spmd, body=%wide.region_0.6_spmd.sunk | while | flops 139250304 | bytes 16645833 | solution.py:88
  805.9 0.9 constant_dynamic-slice_fusion.3
  806.8 1.3 gather_fusion
  808.1 3.1 gather_fusion.1
  811.3 0.1 iota_compare_fusion.4
  811.4 0.9 fusion.91
  812.3 1.1 fusion.92
  813.5 0.4 fusion.93
  813.8 0.1 fusion.94
  814.0 1.0 fusion.95
  815.0 3.1 gather_fusion.2
  818.1 1.3 fusion.96
  819.4 0.9 constant_dynamic-slice_fusion.3
  820.3 1.3 gather_fusion
  821.7 3.1 gather_fusion.1
  824.8 0.1 iota_compare_fusion.4
  824.9 0.9 fusion.91
  825.8 1.1 fusion.92
  827.0 0.4 fusion.93
  827.4 0.1 fusion.94
  827.5 1.0 fusion.95
  828.5 3.1 gather_fusion.2
  831.6 1.3 fusion.96
  832.9 0.9 constant_dynamic-slice_fusion.3
  833.8 1.3 gather_fusion
  835.2 3.1 gather_fusion.1
  838.3 0.1 iota_compare_fusion.4
  838.4 1.0 fusion.91
  839.4 1.1 fusion.92
  840.5 0.4 fusion.93
  840.9 0.1 fusion.94
  841.0 1.0 fusion.95
  842.0 3.1 gather_fusion.2
  845.2 1.3 fusion.96
  846.4 0.9 constant_dynamic-slice_fusion.3
  847.4 1.3 gather_fusion
  848.7 3.1 gather_fusion.1
  851.8 0.1 iota_compare_fusion.4
  851.9 0.9 fusion.91
  852.9 1.1 fusion.92
  854.0 0.4 fusion.93
  854.4 0.1 fusion.94
  854.5 1.0 fusion.95
  855.5 3.1 gather_fusion.2
  858.7 1.3 fusion.96
  859.9 1.2 fusion.65
  861.2 0.8 convert_element_type.20
  862.0 0.0 all-gather.6.cloned.1.call-update
  862.0 0.0 reduce-scatter.2.cloned.1.call-start
  862.1 113.6 %all-gather.6.cloned.1.call-done = bf16[128,4,1024]{2,0,1:T(8,128)(2,1)} async-done(((bf16[32,4,1024]{2,0,1:T(8,128)(2,1)}), bf16[128,4,1024]{2,0,1:T(8,128)(2,1)}) %all-gather.6.cloned.1.call-update) | async-done | bytes 1048592 | tf_op jit(solution)/shard_map/all_gather | solution.py:136
  975.7 6.2 fusion.61
  981.9 0.0 reduce-scatter.2.cloned.1.call-update
  982.0 35.5 %reduce-scatter.2.cloned.1.call-done = bf16[128,4,256]{2,0,1:T(8,128)(2,1)} async-done(((bf16[128,4,2048]{2,0,1:T(8,128)(2,1)}), bf16[128,4,256]{2,0,1:T(8,128)(2,1)}) %reduce-scatter.2.cloned.1.call-update) | async-done | bytes 262160 | tf_op jit(solution)/shard_map/reduce_scatter | solution.py:140
  1017.4 1.9 copy.14
  (40 shorter events, 0.4 us)
Async XLA Ops:
  6.5 1.5 copy-start
  6.5 376.5 %all-gather.8.cloned.1.call-start = ((), (), s32[]{:S(2)}) async-start(), calls=%async_computation.3 | async-start | bytes 4259840 | tf_op jit(solution)/shard_map/all_gather | solution.py:119
  7.3 798.6 %all-gather.10.cloned.1.call-start = ((), (), s32[]{:S(2)}) async-start(), calls=%async_computation.4 | async-start | bytes 4259840 | tf_op jit(solution)/shard_map/all_gather | solution.py:120
  8.0 967.7 %all-gather.6.cloned.1.call-start = ((), (), s32[]{:S(2)}) async-start(), calls=%async_computation.1 | async-start | bytes 1310720 | tf_op jit(solution)/shard_map/all_gather | solution.py:136
  862.0 155.4 %reduce-scatter.2.cloned.1.call-start = ((), (), s32[]{:S(2)}) async-start(), calls=%async_computation.2 | async-start | bytes 2359296 | tf_op jit(solution)/shard_map/reduce_scatter | solution.py:140
Sparse Core Ops, SparseCore 0:
  9.4 373.5 all-gather.7
  385.1 420.7 all-gather.9
  862.2 113.5 all-gather.5
  982.1 35.2 reduce-scatter.1
where the time goes:
time: 1030 us
  waiting for transfers between devices  948 us (92%)
  local copies, waits for them, and re-layouts  36.8 us (4%)
  matrix products  23.4 us (2%)
  between operations  13.2 us (1%)
    all_gather x1, waiting for transfers between devices, local(): lax.all_gather(flat_values, ('group', 'rows'), axis=0, tiled=True)  423 us
    all_gather x1, waiting for transfers between devices, local(): lax.all_gather(flat_keys, ('group', 'rows'), axis=0, tiled=True)  375 us
    all_gather x1, waiting for transfers between devices, local(): attended = lax.all_gather(attended_own, 'rows', axis=0, tiled=True)  114 us
    reduce_scatter x1, waiting for transfers between devices, local(): lax.psum_scatter(head_terms.astype(jnp.bfloat16), 'tensor', scatter_dimen...  35.5 us
  transfers between devices with their start and end apart: 4, of which 4 were waited for; matrix products, arithmetic and copies ran while one was open for 0% of the time, Pallas kernels for 0%

commit v1 on v0

v1 whole, which is shorter than its diff:
```python
import functools
import math

import jax
import jax.numpy as jnp
from jax import lax
from jax.experimental import pallas as pl
from jax.experimental.pallas import tpu as pltpu
from jax.sharding import PartitionSpec as P

MESH = pl.DeviceIdType.MESH
SCALE = 1.0 / math.sqrt(128.0)
F32 = jnp.float32
BF16 = jnp.bfloat16
RP = 4
AP = 4


def place():
    g = lax.axis_index("group")
    return g // 4, lax.axis_index("rows") * 4 + lax.rem(g, 4), lax.axis_index("tensor")


def device(y, z, t):
    y, z, t = lax.rem(y + 4, 4), lax.rem(z + 16, 16), lax.rem(t + 8, 8)
    return (y * 4 + lax.rem(z, 4), z // 4, t)


def dot(a, b, da, db):
    return lax.dot_general(a, b, (((da,), (db,)), ((), ())), preferred_element_type=F32)


def kernel(
    q_hbm, ck_hbm, cv_hbm, pk_hbm, pv_hbm, idx_hbm, lens, w_hbm, out_ref,
    q_in, ck_in, cv_in, pv_in, idx_in, w, kk, vt, qs, rq, qb, top, tot, acc, rs, rr, oht, att, ps, pr,
    load_sem, ring_s, ring_r, q_s, q_r, ret_s, ret_r, ag_s, ag_r, p_s, p_r,
):
    y, z, t = place()
    z_lo, h = lax.rem(z, 4), z // 4

    loads = []
    for n, (src, dst) in enumerate(
        (
            (pk_hbm.at[0], kk.at[0]),
            (pv_hbm.at[0], pv_in),
            (idx_hbm, idx_in),
            (q_hbm, q_in),
            (ck_hbm, ck_in),
            (cv_hbm, cv_in),
            (w_hbm, w),
        )
    ):
        loads.append(pltpu.make_async_copy(src, dst, load_sem.at[n]))
        loads[-1].start()

    barrier = pltpu.get_barrier_semaphore()
    partners = [device(y, z + d, t) for d in (1, -1, 4, -4)]
    partners += [device(y + d, z, t) for d in (1, 2, 3)]
    partners += [device(y, z, t + d) for d in range(1, 8)]
    for who in partners:
        pl.semaphore_signal(barrier, inc=1, device_id=who, device_id_type=MESH)

    def remote(src, dst, send, recv, who):
        return pltpu.make_async_remote_copy(
            src_ref=src, dst_ref=dst, send_sem=send, recv_sem=recv, device_id=who, device_id_type=MESH
        )

    def ring(way, piece, d):
        if way == 0:
            a, b, who = d - 1, d, device(y, z + 1, t)
        else:
            a, b, who = lax.rem(17 - d, 16), 16 - d, device(y, z - 1, t)
        buf, part = (kk, pl.ds(128 * piece, 128)) if piece < 2 else (vt, pl.ds(64 * (piece - 2), 64))
        return remote(buf.at[a, part], buf.at[b, part], ring_s.at[way, piece, d], ring_r.at[way, piece, d], who)

    loads[1].wait()
    vt[0] = jnp.transpose(pv_in[...].astype(F32)).astype(BF16)

    loads[2].wait()
    col = jnp.transpose(jnp.broadcast_to(idx_in[...].astype(F32), (128, 128)))
    i = lax.broadcasted_iota(jnp.int32, (128, 128), 0) - h * 32
    row = lax.broadcasted_iota(jnp.int32, (128, 128), 1) // 4
    mine = jnp.sum(jnp.where(i == row, col, 0.0), axis=0, keepdims=True)
    rank = jnp.sum(jnp.where((col == mine) & (i >= 0) & (i < row), 1.0, 0.0), axis=0, keepdims=True)
    position = lax.rem(lax.broadcasted_iota(jnp.int32, (1, 128), 1), 4).astype(F32)
    slot_row = mine * 16.0 + rank * 4.0 + position
    one_hot = jnp.where(lax.broadcasted_iota(jnp.int32, (256, 128), 0).astype(F32) == slot_row, 1.0, 0.0)
    oht[...] = jnp.transpose(one_hot).astype(BF16)
    one_hot = one_hot.astype(BF16)

    for n in (0, 3, 4, 5):
        loads[n].wait()
    pl.semaphore_wait(barrier, len(partners))
    for piece in range(RP):
        for way in range(2):
            ring(way, piece, 1).start()

    def rows_of(ref):
        return ref[...].astype(F32).reshape(128, ref.shape[2]).astype(BF16)

    qs[:, :, 0:1024] = dot(one_hot, rows_of(q_in), 1, 0).astype(BF16).reshape(4, 64, 1024)
    qs[:, :, 1024:1152] = dot(one_hot, rows_of(ck_in), 1, 0).astype(BF16).reshape(4, 64, 128)
    qs[:, :, 1152:1280] = dot(one_hot, rows_of(cv_in), 1, 0).astype(BF16).reshape(4, 64, 128)
    q_copies = []
    for d in (1, 2, 3):
        q_copies.append(
            remote(qs.at[lax.rem(y + d, 4)], rq.at[y], q_s.at[d], q_r.at[d], device(y + d, z, t))
        )
        q_copies[-1].start()
    rq[y] = qs[y]
    for copy in q_copies:
        copy.wait_recv()

    def begin(rel, _):
        at = pl.ds(pl.multiple_of(lax.rem(z_lo + rel, 4) * 16, 16), 16)
        for g in range(8):
            for source in range(4):
                qb[rel, pl.ds(g * 64 + source * 16, 16), :] = rq[source, at, g * 128 : (g + 1) * 128]
        keys = jnp.concatenate([rq[source, at, 1024:1152] for source in range(4)], axis=0)
        values = jnp.concatenate([rq[source, at, 1152:1280] for source in range(4)], axis=0)
        s = dot(keys, qb[rel], 1, 1)
        key_row = lax.broadcasted_iota(jnp.int32, (64, 512), 0)
        query_row = lax.rem(lax.broadcasted_iota(jnp.int32, (64, 512), 1), 64)
        seen = (key_row // 4 == query_row // 4) & (key_row <= query_row)
        s = jnp.where(seen, s, -1e30)
        peak = jnp.max(s, axis=0, keepdims=True)
        e = jnp.exp((s - peak) * SCALE)
        top[rel] = peak
        tot[rel] = jnp.sum(e, axis=0, keepdims=True)
        acc[rel] = dot(values, e.astype(BF16), 0, 0)
        return 0

    lax.fori_loop(0, 4, begin, 0)

    def attend(k):
        rel = lax.rem(16 - k, 4)
        source = lax.rem(z - k + 16, 16)
        valid = lens[y * 4 + lax.rem(source, 4)] - 256 * (source // 4)
        s = dot(kk[k], qb[rel], 1, 1)
        s = jnp.where(lax.broadcasted_iota(jnp.int32, (256, 512), 0) < valid, s, -1e30)
        before = top[rel]
        peak = jnp.maximum(before, jnp.max(s, axis=0, keepdims=True))
        e = jnp.exp((s - peak) * SCALE)
        fade = jnp.exp((before - peak) * SCALE)
        top[rel] = peak
        tot[rel] = tot[rel] * fade + jnp.sum(e, axis=0, keepdims=True)
        acc[rel] = acc[rel] * fade + dot(vt[k], e.astype(BF16), 1, 0)

    attend(0)

    def step(d, _):
        for piece in range(RP):
            for way in range(2):
                ring(way, piece, d).wait_recv()
                if (piece < 2) == (way == 0):
                    ring(way, piece, d + 1).start()
                else:
                    pl.when(d < 7)(ring(way, piece, d + 1).start)

        def both(j, _):
            attend(jnp.where(j == 0, d, 16 - d))
            return 0

        lax.fori_loop(0, 2, both, 0)
        return 0

    lax.fori_loop(1, 8, step, 0)

    def hand_back(d, rel, at):
        return remote(
            rs.at[lax.rem(y + d, 4), at], rr.at[y, at], ret_s.at[d, rel], ret_r.at[d, rel], device(y + d, z, t)
        )

    def slot_rows(rel):
        return pl.ds(pl.multiple_of(lax.rem(z_lo + rel, 4) * 16, 16), 16)

    def finish(rel, _):
        at = slot_rows(rel)
        o = jnp.transpose(acc[rel] / tot[rel]).astype(BF16)
        for source in range(4):
            for g in range(8):
                lo = g * 64 + source * 16
                rs[source, at, g * 128 : (g + 1) * 128] = o[lo : lo + 16, :]
        for d in (1, 2, 3):
            hand_back(d, rel, at).start()
        rr[y, at, :] = rs[y, at, :]
        return 0

    lax.fori_loop(1, 4, finish, 0)
    for piece in range(RP):
        ring(0 if piece < 2 else 1, piece, 8).wait_recv()
    attend(8)
    finish(0, 0)
    for rel in range(4):
        for d in (1, 2, 3):
            hand_back(d, rel, slot_rows(rel)).wait_recv()

    att[0] = dot(oht[...], rr[...].reshape(256, 1024), 1, 0).astype(BF16)

    def spread(way, piece):
        up, rows = way % 2 == 0, 128 // AP
        if way < 2:
            src, dst, part = 0, 1 if up else 3, pl.ds(piece * rows, rows)
        else:
            src, dst = 1 if up else 3, 2
            part = pl.ds(piece * rows + (0 if up else rows // 2), rows // 2)
        who = device(y, z + 4 if up else z - 4, t)
        return remote(att.at[src, part], att.at[dst, part], ag_s.at[way, piece], ag_r.at[way, piece], who)

    for piece in range(AP):
        for way in range(2):
            spread(way, piece).start()

    loads[6].wait()

    def share(d, number, at):
        return remote(ps.at[d, at], pr.at[d, at], p_s.at[number, d], p_r.at[number, d], device(y, z, t + d))

    def project(a, number, at):
        def column(d, _):
            cols = pl.ds(pl.multiple_of(lax.rem(t + d, 8) * 256, 256), 256)
            part = dot(a, w[:, cols], 1, 0).astype(BF16)

            @pl.when(d < 8)
            def _():
                ps[d, at, :] = part
                share(d, number, at).start()

            @pl.when(d == 8)
            def _():
                pr[0, at, :] = part

            return 0

        lax.fori_loop(1, 9, column, 0)

    spans = [pl.ds(0, 128)]
    project(att[0], 0, spans[0])
    rows = 128 // AP
    for piece in range(AP):
        for way in range(2):
            spread(way, piece).wait_recv()
            spread(way + 2, piece).start()
        spans.append(pl.ds(128 + piece * 2 * rows, 2 * rows))
        lo = piece * rows
        project(jnp.concatenate([att[1, lo : lo + rows], att[3, lo : lo + rows]], axis=0), 1 + piece, spans[-1])
    for piece in range(AP):
        for way in range(2):
            spread(way + 2, piece).wait_recv()
        spans.append(pl.ds(384 + piece * rows, rows))
        project(att[2, piece * rows : (piece + 1) * rows], 1 + AP + piece, spans[-1])

    def result(number, at, pieces):
        for d in range(1, 8):
            share(d, number, at).wait_recv()
        total = pr[0, at, :].astype(F32)
        for d in range(1, 8):
            total = total + pr[d, at, :].astype(F32)
        for below, lo, first, count in pieces:
            home = lax.rem(h - below + 4, 4) * 32 + first // 4
            part = total[lo : lo + count].reshape(count // 4, 4, 256)
            out_ref[pl.ds(home, count // 4)] = part.astype(BF16)

    result(0, spans[0], [(0, 0, 0, 128)])
    for piece in range(AP):
        result(1 + piece, spans[1 + piece], [(1, 0, piece * rows, rows), (3, rows, piece * rows, rows)])
    for piece in range(AP):
        result(1 + AP + piece, spans[1 + AP + piece], [(2, 0, piece * rows, rows)])

    def sent(d, _):
        for piece in range(RP):
            for way in range(2):
                if (piece < 2) == (way == 0):
                    ring(way, piece, d).wait_send()
                else:
                    pl.when(d < 8)(ring(way, piece, d).wait_send)
        return 0

    lax.fori_loop(1, 9, sent, 0)
    for copy in q_copies:
        copy.wait_send()
    for rel in range(4):
        for d in (1, 2, 3):
            hand_back(d, rel, slot_rows(rel)).wait_send()
    for piece in range(AP):
        for way in range(4):
            spread(way, piece).wait_send()
    for number, at in enumerate(spans):
        for d in range(1, 8):
            share(d, number, at).wait_send()


def local(q, ck, cv, pk, pv, index, lens, w):
    dma = pltpu.SemaphoreType.DMA
    anywhere = pl.BlockSpec(memory_space=pl.ANY)
    return pl.pallas_call(
        kernel,
        out_shape=jax.ShapeDtypeStruct((128, 4, 256), BF16),
        in_specs=[anywhere] * 6 + [pl.BlockSpec(memory_space=pltpu.SMEM), anywhere],
        out_specs=pl.BlockSpec(memory_space=pltpu.VMEM),
        scratch_shapes=[
            pltpu.VMEM((32, 4, 1024), BF16),
            pltpu.VMEM((32, 4, 128), BF16),
            pltpu.VMEM((32, 4, 128), BF16),
            pltpu.VMEM((256, 128), BF16),
            pltpu.VMEM((1, 128), jnp.int32),
            pltpu.VMEM((1024, 2048), BF16),
            pltpu.VMEM((16, 256, 128), BF16),
            pltpu.VMEM((16, 128, 256), BF16),
            pltpu.VMEM((4, 64, 1280), BF16),
            pltpu.VMEM((4, 64, 1280), BF16),
            pltpu.VMEM((4, 512, 128), BF16),
            pltpu.VMEM((4, 1, 512), F32),
            pltpu.VMEM((4, 1, 512), F32),
            pltpu.VMEM((4, 128, 512), F32),
            pltpu.VMEM((4, 64, 1024), BF16),
            pltpu.VMEM((4, 64, 1024), BF16),
            pltpu.VMEM((128, 256), BF16),
            pltpu.VMEM((4, 128, 1024), BF16),
            pltpu.VMEM((8, 512, 256), BF16),
            pltpu.VMEM((8, 512, 256), BF16),
            dma((7,)),
            dma((2, RP, 9)),
            dma((2, RP, 9)),
            dma((4,)),
            dma((4,)),
            dma((4, 4)),
            dma((4, 4)),
            dma((4, AP)),
            dma((4, AP)),
            dma((1 + 2 * AP, 8)),
            dma((1 + 2 * AP, 8)),
        ],
        compiler_params=pltpu.CompilerParams(
            collective_id=0, has_side_effects=True, vmem_limit_bytes=48 * 1024 * 1024
        ),
    )(q, ck, cv, pk, pv, index.reshape(1, 128), lens, w)


def solution(mesh):
    return jax.shard_map(
        local,
        mesh=mesh,
        in_specs=(
            P(("group", "rows"), None, "tensor"),
            P(("group", "rows"), None, "tensor"),
            P(("group", "rows"), None, "tensor"),
            P("group", "rows", "tensor"),
            P("group", "rows", "tensor"),
            P("group", None),
            P(),
            P("tensor", "rows"),
        ),
        out_specs=P("group", None, ("rows", "tensor")),
        check_vma=False,
    )
```

time: 1030 us -> 111 us (0.11)
  waiting for transfers between devices: 948 us -> 0 us
  Pallas kernels: 0 us -> 100 us
  local copies, waits for them, and re-layouts: 36.8 us -> 8.34 us
  matrix products: 23.4 us -> 0 us
  between operations: 13.2 us -> 0.02 us
    all_gather x3 -> x0, waiting for transfers between devices: 911 us -> none  [the longest x1 423 us: local(): lax.all_gather(flat_values, ('group', 'rows'), axis=0, tiled=True)]
    pallas_call x0 -> x1, Pallas kernels: none -> 100 us  [local(): pl.pallas_call(kernel, out_shape=jax.ShapeDtypeStruct((128, 4, 256), BF16...]
    reduce_scatter x1 -> x0, waiting for transfers between devices: 35.5 us -> none  [local(): lax.psum_scatter(head_terms.astype(jnp.bfloat16), 'tensor', scatter_dimen...]
    gather x12 -> x0, local copies, waits for them, and re-layouts: 30.3 us -> none  [the longest x4 12.6 us: partial_rows(): jnp.take(value_rows, row_numbers, axis=0)]
    dot_general x17 -> x0, matrix products: 23.4 us -> none  [the longest x1 6.2 us: local(): jnp.dot(flattened, out_weight, preferred_element_type=jnp.float32)]
  transfers between devices with their start and end apart: 4 -> 0, of which waited for: 4 -> 0; matrix products, arithmetic and copies ran while one was open for 0% -> 0% of each run, Pallas kernels for 0% -> 0%
where the time goes in v1:
time: 111 us; the launch traced here: 109 us
  Pallas kernels  100 us (90%)
  local copies, waits for them, and re-layouts  8.34 us (8%)
    pallas_call x1, Pallas kernels, local(): pl.pallas_call(kernel, out_shape=jax.ShapeDtypeStruct((128, 4, 256), BF16...  100 us
    unnamed x17, local copies, waits for them, and re-layouts  8.34 us

profile of v1, /device:TPU:1, one launch (start us, length us, event | category | flops | bytes accessed | tf_op | source)
XLA Modules:
  0.0 108.5 jit_solution(6314455774065223549)
XLA Ops:
  0.0 0.0 copy-start
  0.0 2.2 %copy-done = bf16[1024,2048]{1,0:T(8,128)(2,1)S(1)} copy-done((bf16[1024,2048]{1,0:T(8,128)(2,1)S(1)}, bf16[1024,2048]{1,0:T(8,128)(2,1)}, u32[]{:S(2)}) %copy-start) | copy-done | bytes 4194328
  2.2 0.0 copy-start.1
  2.2 0.9 copy-done.1
  3.1 0.0 copy-start.2
  3.1 0.8 copy-done.2
  4.0 0.0 copy-start.3
  4.0 0.8 copy-done.3
  4.8 0.0 copy-start.4
  4.8 0.8 copy-done.4
  5.6 0.0 copy-start.5
  5.6 0.8 copy-done.5
  6.3 0.0 copy-start.6
  6.3 0.7 copy-done.6
  7.0 0.0 copy-start.7
  7.0 0.7 copy-done.7
  7.6 100.2 %shard_map.82 = bf16[128,4,256]{2,1,0:T(4,128)(2,1)S(1)} custom-call(bf16[32,4,1024]{2,1,0:T(4,128)(2,1)S(1)} %copy-done.1, bf16[32,4,128]{2,1,0:T(4,128)(2,1)S(1)} %copy-done.4, bf16[32,4,128]{2,1,0:T(4,128)(2,1)S(1)} %copy-done.5, bf16[1,256,128]{2,1,0:T(8,128)(2,1)S(1)} %copy-done.2, bf16[1,256,128]{2,1,0:T(8,128)(2,1)S(1)} %copy-done.3, ...), custom_call_target="tpu_custom_call" | custom-call | tf_op jit(solution)/shard_map/pallas_call | solution.py:296
  107.8 0.7 copy.10
Async XLA Ops:
  0.0 2.2 %copy-start = (bf16[1024,2048]{1,0:T(8,128)(2,1)S(1)}, bf16[1024,2048]{1,0:T(8,128)(2,1)}, u32[]{:S(2)}) copy-start(bf16[1024,2048]{1,0:T(8,128)(2,1)} %w_hbm.1) | copy-start | bytes 12582916
  2.2 0.9 copy-start.1
  3.1 0.8 copy-start.2
  4.0 0.8 copy-start.3
  4.8 0.8 copy-start.4
  5.6 0.8 copy-start.5
  6.3 0.7 copy-start.6
  7.0 0.7 copy-start.7

commit v2 on v1

--- a/solution.py
+++ b/solution.py
@@ -70,8 +70,12 @@
             a, b, who = d - 1, d, device(y, z + 1, t)
         else:
             a, b, who = lax.rem(17 - d, 16), 16 - d, device(y, z - 1, t)
-        buf, part = (kk, pl.ds(128 * piece, 128)) if piece < 2 else (vt, pl.ds(64 * (piece - 2), 64))
-        return remote(buf.at[a, part], buf.at[b, part], ring_s.at[way, piece, d], ring_r.at[way, piece, d], who)
+        n = piece % (RP // 2)
+        if piece < RP // 2:
+            buf, part = kk, pl.ds(n * (512 // RP), 512 // RP)
+        else:
+            buf, part = vt, pl.ds(n * (256 // RP), 256 // RP)
+        return remote(buf.at[a, part], buf.at[b, part], ring_s.at[piece // (RP // 2)], ring_r.at[way, piece, d], who)
 
     loads[1].wait()
     vt[0] = jnp.transpose(pv_in[...].astype(F32)).astype(BF16)
@@ -88,12 +92,13 @@
     oht[...] = jnp.transpose(one_hot).astype(BF16)
     one_hot = one_hot.astype(BF16)
 
-    for n in (0, 3, 4, 5):
-        loads[n].wait()
+    loads[0].wait()
     pl.semaphore_wait(barrier, len(partners))
     for piece in range(RP):
         for way in range(2):
             ring(way, piece, 1).start()
+    for n in (3, 4, 5):
+        loads[n].wait()
 
     def rows_of(ref):
         return ref[...].astype(F32).reshape(128, ref.shape[2]).astype(BF16)
@@ -104,12 +109,10 @@
     q_copies = []
     for d in (1, 2, 3):
         q_copies.append(
-            remote(qs.at[lax.rem(y + d, 4)], rq.at[y], q_s.at[d], q_r.at[d], device(y + d, z, t))
+            remote(qs.at[lax.rem(y + d, 4)], rq.at[y], q_s.at[0], q_r.at[0], device(y + d, z, t))
         )
         q_copies[-1].start()
     rq[y] = qs[y]
-    for copy in q_copies:
-        copy.wait_recv()
 
     def begin(rel, _):
         at = pl.ds(pl.multiple_of(lax.rem(z_lo + rel, 4) * 16, 16), 16)
@@ -130,8 +133,6 @@
         acc[rel] = dot(values, e.astype(BF16), 0, 0)
         return 0
 
-    lax.fori_loop(0, 4, begin, 0)
-
     def attend(k):
         rel = lax.rem(16 - k, 4)
         source = lax.rem(z - k + 16, 16)
@@ -146,29 +147,36 @@
         tot[rel] = tot[rel] * fade + jnp.sum(e, axis=0, keepdims=True)
         acc[rel] = acc[rel] * fade + dot(vt[k], e.astype(BF16), 1, 0)
 
-    attend(0)
-
-    def step(d, _):
+    def forward(d):
         for piece in range(RP):
             for way in range(2):
                 ring(way, piece, d).wait_recv()
-                if (piece < 2) == (way == 0):
+                if (piece < RP // 2) == (way == 0):
                     ring(way, piece, d + 1).start()
                 else:
                     pl.when(d < 7)(ring(way, piece, d + 1).start)
 
+    def pair(d, _):
         def both(j, _):
             attend(jnp.where(j == 0, d, 16 - d))
             return 0
 
-        lax.fori_loop(0, 2, both, 0)
-        return 0
-
-    lax.fori_loop(1, 8, step, 0)
+        return lax.fori_loop(0, 2, both, 0)
+
+    def step(d, _):
+        forward(d)
+        return pair(d - 2, 0)
+
+    lax.fori_loop(1, 3, lambda d, _: forward(d) or 0, 0)
+    remote(rq.at[0:3], rq.at[0:3], q_s.at[0], q_r.at[0], device(y, z, t)).wait_recv()
+    lax.fori_loop(0, 4, begin, 0)
+    attend(0)
+    lax.fori_loop(3, 8, step, 0)
+    lax.fori_loop(6, 8, pair, 0)
 
     def hand_back(d, rel, at):
         return remote(
-            rs.at[lax.rem(y + d, 4), at], rr.at[y, at], ret_s.at[d, rel], ret_r.at[d, rel], device(y + d, z, t)
+            rs.at[lax.rem(y + d, 4), at], rr.at[y, at], ret_s.at[0], ret_r.at[rel], device(y + d, z, t)
         )
 
     def slot_rows(rel):
@@ -188,12 +196,12 @@
 
     lax.fori_loop(1, 4, finish, 0)
     for piece in range(RP):
-        ring(0 if piece < 2 else 1, piece, 8).wait_recv()
+        ring(0 if piece < RP // 2 else 1, piece, 8).wait_recv()
     attend(8)
     finish(0, 0)
     for rel in range(4):
-        for d in (1, 2, 3):
-            hand_back(d, rel, slot_rows(rel)).wait_recv()
+        some = rr.at[0:3, slot_rows(rel)]
+        remote(some, some, ret_s.at[0], ret_r.at[rel], device(y, z, t)).wait_recv()
 
     att[0] = dot(oht[...], rr[...].reshape(256, 1024), 1, 0).astype(BF16)
 
@@ -205,7 +213,7 @@
             src, dst = 1 if up else 3, 2
             part = pl.ds(piece * rows + (0 if up else rows // 2), rows // 2)
         who = device(y, z + 4 if up else z - 4, t)
-        return remote(att.at[src, part], att.at[dst, part], ag_s.at[way, piece], ag_r.at[way, piece], who)
+        return remote(att.at[src, part], att.at[dst, part], ag_s.at[0], ag_r.at[way, piece], who)
 
     for piece in range(AP):
         for way in range(2):
@@ -214,7 +222,7 @@
     loads[6].wait()
 
     def share(d, number, at):
-        return remote(ps.at[d, at], pr.at[d, at], p_s.at[number, d], p_r.at[number, d], device(y, z, t + d))
+        return remote(ps.at[d, at], pr.at[d, at], p_s.at[0], p_r.at[number], device(y, z, t + d))
 
     def project(a, number, at):
         def column(d, _):
@@ -244,15 +252,10 @@
         spans.append(pl.ds(128 + piece * 2 * rows, 2 * rows))
         lo = piece * rows
         project(jnp.concatenate([att[1, lo : lo + rows], att[3, lo : lo + rows]], axis=0), 1 + piece, spans[-1])
-    for piece in range(AP):
-        for way in range(2):
-            spread(way + 2, piece).wait_recv()
-        spans.append(pl.ds(384 + piece * rows, rows))
-        project(att[2, piece * rows : (piece + 1) * rows], 1 + AP + piece, spans[-1])
 
     def result(number, at, pieces):
-        for d in range(1, 8):
-            share(d, number, at).wait_recv()
+        others = pr.at[1:8, at]
+        remote(others, others, p_s.at[0], p_r.at[number], device(y, z, t)).wait_recv()
         total = pr[0, at, :].astype(F32)
         for d in range(1, 8):
             total = total + pr[d, at, :].astype(F32)
@@ -261,33 +264,33 @@
             part = total[lo : lo + count].reshape(count // 4, 4, 256)
             out_ref[pl.ds(home, count // 4)] = part.astype(BF16)
 
+    def near(piece):
+        result(1 + piece, spans[1 + piece], [(1, 0, piece * rows, rows), (3, rows, piece * rows, rows)])
+
+    def far(piece):
+        result(1 + AP + piece, spans[1 + AP + piece], [(2, 0, piece * rows, rows)])
+
     result(0, spans[0], [(0, 0, 0, 128)])
     for piece in range(AP):
-        result(1 + piece, spans[1 + piece], [(1, 0, piece * rows, rows), (3, rows, piece * rows, rows)])
+        if piece == AP - 1:
+            for n in range(AP):
+                near(n)
+        for way in range(2):
+            spread(way + 2, piece).wait_recv()
+        spans.append(pl.ds(384 + piece * rows, rows))
+        project(att[2, piece * rows : (piece + 1) * rows], 1 + AP + piece, spans[-1])
     for piece in range(AP):
-        result(1 + AP + piece, spans[1 + AP + piece], [(2, 0, piece * rows, rows)])
-
-    def sent(d, _):
-        for piece in range(RP):
-            for way in range(2):
-                if (piece < 2) == (way == 0):
-                    ring(way, piece, d).wait_send()
-                else:
-                    pl.when(d < 8)(ring(way, piece, d).wait_send)
-        return 0
-
-    lax.fori_loop(1, 9, sent, 0)
-    for copy in q_copies:
-        copy.wait_send()
-    for rel in range(4):
-        for d in (1, 2, 3):
-            hand_back(d, rel, slot_rows(rel)).wait_send()
-    for piece in range(AP):
-        for way in range(4):
-            spread(way, piece).wait_send()
-    for number, at in enumerate(spans):
-        for d in range(1, 8):
-            share(d, number, at).wait_send()
+        far(piece)
+
+    for ref, sem in (
+        (kk.at[0:15], ring_s.at[0]),
+        (vt.at[0:15], ring_s.at[1]),
+        (qs.at[0:3], q_s.at[0]),
+        (rs.at[0:3], ret_s.at[0]),
+        (att.at[0:3], ag_s.at[0]),
+        (ps.at[1:8], p_s.at[0]),
+    ):
+        remote(ref, ref, sem, p_r.at[0], device(y, z, t)).wait_send()
 
 
 def local(q, ck, cv, pk, pv, index, lens, w):
@@ -320,19 +323,19 @@
             pltpu.VMEM((8, 512, 256), BF16),
             pltpu.VMEM((8, 512, 256), BF16),
             dma((7,)),
+            dma((2,)),
             dma((2, RP, 9)),
-            dma((2, RP, 9)),
+            dma((1,)),
+            dma((1,)),
+            dma((1,)),
             dma((4,)),
-            dma((4,)),
-            dma((4, 4)),
-            dma((4, 4)),
+            dma((1,)),
             dma((4, AP)),
-            dma((4, AP)),
-            dma((1 + 2 * AP, 8)),
-            dma((1 + 2 * AP, 8)),
+            dma((1,)),
+            dma((1 + 2 * AP,)),
         ],
         compiler_params=pltpu.CompilerParams(
-            collective_id=0, has_side_effects=True, vmem_limit_bytes=48 * 1024 * 1024
+            collective_id=0, has_side_effects=True, vmem_limit_bytes=63 * 1024 * 1024
         ),
     )(q, ck, cv, pk, pv, index.reshape(1, 128), lens, w)
 

time: 111 us -> 97.6 us (0.88); the launches traced: 109 us -> 97.5 us
  local copies, waits for them, and re-layouts: 8.34 us -> 1.74 us
  Pallas kernels: 100 us -> 95.7 us
    unnamed x17 -> x1, local copies, waits for them, and re-layouts: 8.34 us -> 1.74 us
    pallas_call x1, Pallas kernels: 100 us -> 95.7 us  [local(): pl.pallas_call(kernel, out_shape=jax.ShapeDtypeStruct((128, 4, 256), BF16...]
where the time goes in v2:
time: 97.6 us; the launch traced here: 97.5 us
  Pallas kernels  95.7 us (98%)
  local copies, waits for them, and re-layouts  1.74 us (2%)
    pallas_call x1, Pallas kernels, local(): pl.pallas_call(kernel, out_shape=jax.ShapeDtypeStruct((128, 4, 256), BF16...  95.7 us

profile of v2, /device:TPU:1, one launch (start us, length us, event | category | flops | bytes accessed | tf_op | source)
XLA Modules:
  0.0 97.5 jit_solution(1118585532096547975)
XLA Ops:
  0.0 95.7 %shard_map.82 = bf16[128,4,256]{2,1,0:T(4,128)(2,1)} custom-call(bf16[32,4,1024]{2,1,0:T(4,128)(2,1)} %q_hbm.1, bf16[32,4,128]{2,1,0:T(4,128)(2,1)} %ck_hbm.1, bf16[32,4,128]{2,1,0:T(4,128)(2,1)} %cv_hbm.1, bf16[1,256,128]{2,1,0:T(8,128)(2,1)} %pk_hbm.1, bf16[1,256,128]{2,1,0:T(8,128)(2,1)} %pv_hbm.1, s32[1,128]{1,0:T(1,128)} %bitcast.1, s32[16]{0:T(128)} %lens.1, ...), custom_call_target="tpu_custom_call" | custom-call | tf_op jit(solution)/shard_map/pallas_call | solution.py:299
  95.7 1.7 %copy.10 = bf16[128,4,256]{2,1,0:T(4,128)(2,1)} copy(bf16[128,4,256]{2,1,0:T(4,128)(2,1)} %shard_map.82) | data formatting | bytes 524288

commit v3 on v2

--- a/solution.py
+++ b/solution.py
@@ -31,12 +31,19 @@
 
 
 def kernel(
-    q_hbm, ck_hbm, cv_hbm, pk_hbm, pv_hbm, idx_hbm, lens, w_hbm, out_ref,
-    q_in, ck_in, cv_in, pv_in, idx_in, w, kk, vt, qs, rq, qb, top, tot, acc, rs, rr, oht, att, ps, pr,
+    q_hbm, ck_hbm, cv_hbm, pk_hbm, pv_hbm, idx_hbm, lens_hbm, w_hbm, out_ref,
+    lens, q_in, ck_in, cv_in, pv_in, idx_in, w, kk, vt, qs, rq, qb, top, tot, acc, rs, rr, oht, part_sum, att, ps, pr,
     load_sem, ring_s, ring_r, q_s, q_r, ret_s, ret_r, ag_s, ag_r, p_s, p_r,
 ):
     y, z, t = place()
     z_lo, h = lax.rem(z, 4), z // 4
+
+    barrier = pltpu.get_barrier_semaphore()
+    partners = [device(y, z + d, t) for d in (1, -1, 4, -4)]
+    partners += [device(y + d, z, t) for d in (1, 2, 3)]
+    partners += [device(y, z, t + d) for d in range(1, 8)]
+    for who in partners:
+        pl.semaphore_signal(barrier, inc=1, device_id=who, device_id_type=MESH)
 
     loads = []
     for n, (src, dst) in enumerate(
@@ -47,18 +54,12 @@
             (q_hbm, q_in),
             (ck_hbm, ck_in),
             (cv_hbm, cv_in),
+            (lens_hbm, lens),
             (w_hbm, w),
         )
     ):
         loads.append(pltpu.make_async_copy(src, dst, load_sem.at[n]))
         loads[-1].start()
-
-    barrier = pltpu.get_barrier_semaphore()
-    partners = [device(y, z + d, t) for d in (1, -1, 4, -4)]
-    partners += [device(y + d, z, t) for d in (1, 2, 3)]
-    partners += [device(y, z, t + d) for d in range(1, 8)]
-    for who in partners:
-        pl.semaphore_signal(barrier, inc=1, device_id=who, device_id_type=MESH)
 
     def remote(src, dst, send, recv, who):
         return pltpu.make_async_remote_copy(
@@ -80,6 +81,12 @@
     loads[1].wait()
     vt[0] = jnp.transpose(pv_in[...].astype(F32)).astype(BF16)
 
+    loads[0].wait()
+    pl.semaphore_wait(barrier, len(partners))
+    for piece in range(RP):
+        for way in range(2):
+            ring(way, piece, 1).start()
+
     loads[2].wait()
     col = jnp.transpose(jnp.broadcast_to(idx_in[...].astype(F32), (128, 128)))
     i = lax.broadcasted_iota(jnp.int32, (128, 128), 0) - h * 32
@@ -88,16 +95,9 @@
     rank = jnp.sum(jnp.where((col == mine) & (i >= 0) & (i < row), 1.0, 0.0), axis=0, keepdims=True)
     position = lax.rem(lax.broadcasted_iota(jnp.int32, (1, 128), 1), 4).astype(F32)
     slot_row = mine * 16.0 + rank * 4.0 + position
-    one_hot = jnp.where(lax.broadcasted_iota(jnp.int32, (256, 128), 0).astype(F32) == slot_row, 1.0, 0.0)
-    oht[...] = jnp.transpose(one_hot).astype(BF16)
-    one_hot = one_hot.astype(BF16)
-
-    loads[0].wait()
-    pl.semaphore_wait(barrier, len(partners))
-    for piece in range(RP):
-        for way in range(2):
-            ring(way, piece, 1).start()
-    for n in (3, 4, 5):
+    one_hot = jnp.where(lax.broadcasted_iota(jnp.int32, (256, 128), 0).astype(F32) == slot_row, 1.0, 0.0).astype(BF16)
+
+    for n in (3, 4, 5, 6):
         loads[n].wait()
 
     def rows_of(ref):
@@ -147,8 +147,8 @@
         tot[rel] = tot[rel] * fade + jnp.sum(e, axis=0, keepdims=True)
         acc[rel] = acc[rel] * fade + dot(vt[k], e.astype(BF16), 1, 0)
 
-    def forward(d):
-        for piece in range(RP):
+    def forward(d, half):
+        for piece in range(half * RP // 2, (half + 1) * RP // 2):
             for way in range(2):
                 ring(way, piece, d).wait_recv()
                 if (piece < RP // 2) == (way == 0):
@@ -164,10 +164,23 @@
         return lax.fori_loop(0, 2, both, 0)
 
     def step(d, _):
-        forward(d)
-        return pair(d - 2, 0)
-
-    lax.fori_loop(1, 3, lambda d, _: forward(d) or 0, 0)
+        forward(d, 0)
+        attend(d - 2)
+        forward(d, 1)
+        attend(18 - d)
+        return 0
+
+    forward(1, 0)
+    forward(1, 1)
+    plane = jnp.floor(mine * 0.25)
+    column_of = plane * 16.0 + rank * 4.0 + position
+    below = mine - plane * 4.0
+    for rel in range(4):
+        here = lax.rem(z_lo + rel, 4).astype(F32)
+        hit = (lax.broadcasted_iota(jnp.int32, (64, 128), 0).astype(F32) == column_of) & (below == here)
+        oht[rel] = jnp.transpose(jnp.where(hit, 1.0, 0.0)).astype(BF16)
+    forward(2, 0)
+    forward(2, 1)
     remote(rq.at[0:3], rq.at[0:3], q_s.at[0], q_r.at[0], device(y, z, t)).wait_recv()
     lax.fori_loop(0, 4, begin, 0)
     attend(0)
@@ -199,12 +212,6 @@
         ring(0 if piece < RP // 2 else 1, piece, 8).wait_recv()
     attend(8)
     finish(0, 0)
-    for rel in range(4):
-        some = rr.at[0:3, slot_rows(rel)]
-        remote(some, some, ret_s.at[0], ret_r.at[rel], device(y, z, t)).wait_recv()
-
-    att[0] = dot(oht[...], rr[...].reshape(256, 1024), 1, 0).astype(BF16)
-
     def spread(way, piece):
         up, rows = way % 2 == 0, 128 // AP
         if way < 2:
@@ -215,11 +222,26 @@
         who = device(y, z + 4 if up else z - 4, t)
         return remote(att.at[src, part], att.at[dst, part], ag_s.at[0], ag_r.at[way, piece], who)
 
-    for piece in range(AP):
+    def returned(rel):
+        some = rr.at[0:3, slot_rows(rel)]
+        remote(some, some, ret_s.at[0], ret_r.at[rel], device(y, z, t)).wait_recv()
+        return jnp.concatenate([rr[source, slot_rows(rel), :] for source in range(4)], axis=0)
+
+    def unpack(rel, _):
+        part_sum[...] += dot(oht[rel], returned(rel), 1, 0)
+        return 0
+
+    part_sum[...] = dot(oht[1], returned(1), 1, 0)
+    lax.fori_loop(2, 4, unpack, 0)
+    last = returned(0)
+    rows = 128 // AP
+    for piece in range(AP):
+        at = slice(piece * rows, (piece + 1) * rows)
+        att[0, at] = (part_sum[at] + dot(oht[0, at], last, 1, 0)).astype(BF16)
         for way in range(2):
             spread(way, piece).start()
 
-    loads[6].wait()
+    loads[7].wait()
 
     def share(d, number, at):
         return remote(ps.at[d, at], pr.at[d, at], p_s.at[0], p_r.at[number], device(y, z, t + d))
@@ -244,7 +266,6 @@
 
     spans = [pl.ds(0, 128)]
     project(att[0], 0, spans[0])
-    rows = 128 // AP
     for piece in range(AP):
         for way in range(2):
             spread(way, piece).wait_recv()
@@ -270,15 +291,14 @@
     def far(piece):
         result(1 + AP + piece, spans[1 + AP + piece], [(2, 0, piece * rows, rows)])
 
-    result(0, spans[0], [(0, 0, 0, 128)])
-    for piece in range(AP):
-        if piece == AP - 1:
-            for n in range(AP):
-                near(n)
+    for piece in range(AP):
         for way in range(2):
             spread(way + 2, piece).wait_recv()
         spans.append(pl.ds(384 + piece * rows, rows))
         project(att[2, piece * rows : (piece + 1) * rows], 1 + AP + piece, spans[-1])
+    result(0, spans[0], [(0, 0, 0, 128)])
+    for piece in range(AP):
+        near(piece)
     for piece in range(AP):
         far(piece)
 
@@ -295,13 +315,14 @@
 
 def local(q, ck, cv, pk, pv, index, lens, w):
     dma = pltpu.SemaphoreType.DMA
-    anywhere = pl.BlockSpec(memory_space=pl.ANY)
+    hbm = pl.BlockSpec(memory_space=pltpu.HBM)
     return pl.pallas_call(
         kernel,
-        out_shape=jax.ShapeDtypeStruct((128, 4, 256), BF16),
-        in_specs=[anywhere] * 6 + [pl.BlockSpec(memory_space=pltpu.SMEM), anywhere],
+        out_shape=pltpu.VMEM((128, 4, 256), BF16),
+        in_specs=[hbm] * 8,
         out_specs=pl.BlockSpec(memory_space=pltpu.VMEM),
         scratch_shapes=[
+            pltpu.SMEM((16,), jnp.int32),
             pltpu.VMEM((32, 4, 1024), BF16),
             pltpu.VMEM((32, 4, 128), BF16),
             pltpu.VMEM((32, 4, 128), BF16),
@@ -318,11 +339,12 @@
             pltpu.VMEM((4, 128, 512), F32),
             pltpu.VMEM((4, 64, 1024), BF16),
             pltpu.VMEM((4, 64, 1024), BF16),
-            pltpu.VMEM((128, 256), BF16),
+            pltpu.VMEM((4, 128, 64), BF16),
+            pltpu.VMEM((128, 1024), F32),
             pltpu.VMEM((4, 128, 1024), BF16),
             pltpu.VMEM((8, 512, 256), BF16),
             pltpu.VMEM((8, 512, 256), BF16),
-            dma((7,)),
+            dma((8,)),
             dma((2,)),
             dma((2, RP, 9)),
             dma((1,)),
@@ -335,7 +357,7 @@
             dma((1 + 2 * AP,)),
         ],
         compiler_params=pltpu.CompilerParams(
-            collective_id=0, has_side_effects=True, vmem_limit_bytes=63 * 1024 * 1024
+            collective_id=0, has_side_effects=True, vmem_limit_bytes=56 * 1024 * 1024
         ),
     )(q, ck, cv, pk, pv, index.reshape(1, 128), lens, w)
 

time: 97.6 us -> 93.8 us (0.961)
  Pallas kernels: 95.7 us -> 93 us
  local copies, waits for them, and re-layouts: 1.74 us -> 0.71 us
    pallas_call x1, Pallas kernels: 95.7 us -> 93 us  [local(): pl.pallas_call(kernel, out_shape=pltpu.VMEM((128, 4, 256), BF16), in_spec...]
    unnamed x1, local copies, waits for them, and re-layouts: 1.74 us -> 0.71 us
where the time goes in v3:
time: 93.8 us; the launch traced here: 93.7 us
  Pallas kernels  93 us (99%)
    pallas_call x1, Pallas kernels, local(): pl.pallas_call(kernel, out_shape=pltpu.VMEM((128, 4, 256), BF16), in_spec...  93 us

profile of v3, /device:TPU:1, one launch (start us, length us, event | category | flops | bytes accessed | tf_op | source)
XLA Modules:
  0.0 93.7 jit_solution(8253665378096277)
XLA Ops:
  0.0 93.0 %shard_map.82 = bf16[128,4,256]{2,1,0:T(4,128)(2,1)S(1)} custom-call(bf16[32,4,1024]{2,1,0:T(4,128)(2,1)} %q_hbm.1, bf16[32,4,128]{2,1,0:T(4,128)(2,1)} %ck_hbm.1, bf16[32,4,128]{2,1,0:T(4,128)(2,1)} %cv_hbm.1, bf16[1,256,128]{2,1,0:T(8,128)(2,1)} %pk_hbm.1, bf16[1,256,128]{2,1,0:T(8,128)(2,1)} %pv_hbm.1, s32[1,128]{1,0:T(1,128)} %bitcast.1, s32[16]{0:T(128)} %lens_hbm.1, ...), custom_call_target="tpu_custom_call" | custom-call | tf_op jit(solution)/shard_map/pallas_call | solution.py:319
  93.0 0.7 copy.10

commit v4 on v3

--- a/solution.py
+++ b/solution.py
@@ -156,18 +156,15 @@
                 else:
                     pl.when(d < 7)(ring(way, piece, d + 1).start)
 
-    def pair(d, _):
-        def both(j, _):
-            attend(jnp.where(j == 0, d, 16 - d))
-            return 0
-
-        return lax.fori_loop(0, 2, both, 0)
+    def next_chunk(n):
+        attend(jnp.where(n % 2 == 1, (n + 1) // 2, lax.rem(16 - n // 2, 16)))
 
     def step(d, _):
         forward(d, 0)
-        attend(d - 2)
+        next_chunk(3 * d - 9)
         forward(d, 1)
-        attend(18 - d)
+        next_chunk(3 * d - 8)
+        next_chunk(3 * d - 7)
         return 0
 
     forward(1, 0)
@@ -183,9 +180,7 @@
     forward(2, 1)
     remote(rq.at[0:3], rq.at[0:3], q_s.at[0], q_r.at[0], device(y, z, t)).wait_recv()
     lax.fori_loop(0, 4, begin, 0)
-    attend(0)
     lax.fori_loop(3, 8, step, 0)
-    lax.fori_loop(6, 8, pair, 0)
 
     def hand_back(d, rel, at):
         return remote(
@@ -247,22 +242,23 @@
         return remote(ps.at[d, at], pr.at[d, at], p_s.at[0], p_r.at[number], device(y, z, t + d))
 
     def project(a, number, at):
-        def column(d, _):
+        def column(n, _):
+            d = 4 + jnp.where(n % 2 == 0, n // 2, -((n + 1) // 2))
             cols = pl.ds(pl.multiple_of(lax.rem(t + d, 8) * 256, 256), 256)
             part = dot(a, w[:, cols], 1, 0).astype(BF16)
 
-            @pl.when(d < 8)
+            @pl.when(d > 0)
             def _():
                 ps[d, at, :] = part
                 share(d, number, at).start()
 
-            @pl.when(d == 8)
+            @pl.when(d == 0)
             def _():
                 pr[0, at, :] = part
 
             return 0
 
-        lax.fori_loop(1, 9, column, 0)
+        lax.fori_loop(0, 8, column, 0)
 
     spans = [pl.ds(0, 128)]
     project(att[0], 0, spans[0])

time: 93.8 us -> 91.2 us (0.972)
  Pallas kernels: 93 us -> 90.4 us
    pallas_call x1, Pallas kernels: 93 us -> 90.4 us  [local(): pl.pallas_call(kernel, out_shape=pltpu.VMEM((128, 4, 256), BF16), in_spec...]
where the time goes in v4:
time: 91.2 us; the launch traced here: 91.1 us
  Pallas kernels  90.4 us (99%)
    pallas_call x1, Pallas kernels, local(): pl.pallas_call(kernel, out_shape=pltpu.VMEM((128, 4, 256), BF16), in_spec...  90.4 us

profile of v4, /device:TPU:1, one launch (start us, length us, event | category | flops | bytes accessed | tf_op | source)
XLA Modules:
  0.0 91.1 jit_solution(5763435830907553506)
XLA Ops:
  0.0 90.4 %shard_map.82 = bf16[128,4,256]{2,1,0:T(4,128)(2,1)S(1)} custom-call(bf16[32,4,1024]{2,1,0:T(4,128)(2,1)} %q_hbm.1, bf16[32,4,128]{2,1,0:T(4,128)(2,1)} %ck_hbm.1, bf16[32,4,128]{2,1,0:T(4,128)(2,1)} %cv_hbm.1, bf16[1,256,128]{2,1,0:T(8,128)(2,1)} %pk_hbm.1, bf16[1,256,128]{2,1,0:T(8,128)(2,1)} %pv_hbm.1, s32[1,128]{1,0:T(1,128)} %bitcast.1, s32[16]{0:T(128)} %lens_hbm.1, ...), custom_call_target="tpu_custom_call" | custom-call | tf_op jit(solution)/shard_map/pallas_call | solution.py:315
  90.4 0.7 copy.10

commit v5 on v4

--- a/solution.py
+++ b/solution.py
@@ -167,8 +167,7 @@
         next_chunk(3 * d - 7)
         return 0
 
-    forward(1, 0)
-    forward(1, 1)
+    lax.fori_loop(1, 3, lambda d, _: forward(d, 0) or forward(d, 1) or 0, 0)
     plane = jnp.floor(mine * 0.25)
     column_of = plane * 16.0 + rank * 4.0 + position
     below = mine - plane * 4.0
@@ -176,8 +175,6 @@
         here = lax.rem(z_lo + rel, 4).astype(F32)
         hit = (lax.broadcasted_iota(jnp.int32, (64, 128), 0).astype(F32) == column_of) & (below == here)
         oht[rel] = jnp.transpose(jnp.where(hit, 1.0, 0.0)).astype(BF16)
-    forward(2, 0)
-    forward(2, 1)
     remote(rq.at[0:3], rq.at[0:3], q_s.at[0], q_r.at[0], device(y, z, t)).wait_recv()
     lax.fori_loop(0, 4, begin, 0)
     lax.fori_loop(3, 8, step, 0)
@@ -197,7 +194,7 @@
             for g in range(8):
                 lo = g * 64 + source * 16
                 rs[source, at, g * 128 : (g + 1) * 128] = o[lo : lo + 16, :]
-        for d in (1, 2, 3):
+        for d in (2, 1, 3):
             hand_back(d, rel, at).start()
         rr[y, at, :] = rs[y, at, :]
         return 0

time: 91.2 us -> 91.7 us (level)
  no operation moved by 1% of the time
where the time goes in v5:
time: 91.7 us; the launch traced here: 91.6 us
  Pallas kernels  90.9 us (99%)
    pallas_call x1, Pallas kernels, local(): pl.pallas_call(kernel, out_shape=pltpu.VMEM((128, 4, 256), BF16), in_spec...  90.9 us

profile of v5, /device:TPU:1, one launch (start us, length us, event | category | flops | bytes accessed | tf_op | source)
XLA Modules:
  0.0 91.6 jit_solution(11421662375347456514)
XLA Ops:
  0.0 90.9 %shard_map.82 = bf16[128,4,256]{2,1,0:T(4,128)(2,1)S(1)} custom-call(bf16[32,4,1024]{2,1,0:T(4,128)(2,1)} %q_hbm.1, bf16[32,4,128]{2,1,0:T(4,128)(2,1)} %ck_hbm.1, bf16[32,4,128]{2,1,0:T(4,128)(2,1)} %cv_hbm.1, bf16[1,256,128]{2,1,0:T(8,128)(2,1)} %pk_hbm.1, bf16[1,256,128]{2,1,0:T(8,128)(2,1)} %pv_hbm.1, s32[1,128]{1,0:T(1,128)} %bitcast.1, s32[16]{0:T(128)} %lens_hbm.1, ...), custom_call_target="tpu_custom_call" | custom-call | tf_op jit(solution)/shard_map/pallas_call | solution.py:312
  90.9 0.7 copy.10
